TPU v7x, 512 devices: a whole 4x8x8 slice. The times are simulated.
512 devices in a mesh: row: 16 (over y, core), col: 32 (over x, z).
Axes of the slice: x: 4, y: 8, z: 8, core: 2. Of those that a mesh axis runs over, the one named last changes fastest.
Arguments:
- lam: float32 [14400, 2400], P('row', 'col'), may hold values from -6 to 6
- cycle: float32 [2400, 24000], P('row', 'col'), may hold values from -0.125 to 0.125
- eps_occ: float32 [200], replicated, may hold values from -2 to -0.3
- eps_vir: float32 [1200], replicated, may hold values from 0.1 to 3
- occ_irrep: int32 [200], replicated, may hold values from 0 to 7
- slab: int32 [12], replicated, may hold values from 0 to 199, as said below
- pair_occ: int32 [20], replicated, may hold values from 0 to 199, as said below
- irrep_start: int32 [8], replicated, may hold values from 0 to 1125, as said below
Outputs:
- update: float32 [14400, 24000], P('row', 'col')
Inputs may be any that keep to these rules, and one draw needn't show every extreme that they name: `irrep_start`: entry 0 is 0 and the entries rise strictly, so each irrep holds one or more virtual orbitals; the last entry is 1125; sizes may differ. `slab`: distinct occupied orbitals. `pair_occ`: distinct occupied orbitals.
All inputs are finite; a program needn't handle non-finite values.
Results may differ from a plain program's by a relative error of at most 0.000073.
Values sent between devices are 32-bit elements; how exact they have to be, the bound alone decides.
A program may use at most 128 MiB of HBM per device.

v0:
```python
import jax
import jax.numpy as jnp
from jax import lax
from jax.sharding import PartitionSpec as P

V = 1200


def irrep_of(index, starts):
    return jnp.sum((index[:, None] >= starts[None, :]).astype(jnp.int32), axis=1) - 1


def local(lam, cycle, eps_occ, eps_vir, occ_irrep, slab, pair_occ, irrep_start):
    row_count = lam.shape[0]
    col_count = cycle.shape[1]
    cycle_full = lax.all_gather(cycle, "row", axis=0, tiled=True)
    prod = jnp.dot(
        lax.all_gather(lam, "col", axis=1, tiled=True),
        cycle_full,
        precision=lax.Precision.HIGHEST,
        preferred_element_type=jnp.float32,
    )
    rows = lax.axis_index("row") * row_count + jnp.arange(row_count, dtype=jnp.int32)
    cols = lax.axis_index("col") * col_count + jnp.arange(col_count, dtype=jnp.int32)
    occ_row = jnp.take(slab, rows // V)
    vir_row = rows % V
    occ_col = jnp.take(pair_occ, cols // V)
    vir_col = cols % V
    row_energy = jnp.take(eps_occ, occ_row) - jnp.take(eps_vir, vir_row)
    col_energy = jnp.take(eps_occ, occ_col) - jnp.take(eps_vir, vir_col)
    row_sym = jnp.bitwise_xor(jnp.take(occ_irrep, occ_row), irrep_of(vir_row, irrep_start))
    col_sym = jnp.bitwise_xor(jnp.take(occ_irrep, occ_col), irrep_of(vir_col, irrep_start))
    allowed = row_sym[:, None] == col_sym[None, :]
    denom = row_energy[:, None] + col_energy[None, :]
    return jnp.where(allowed, prod / denom, jnp.float32(0.0))


def solution(mesh):
    placed = (P("row", "col"), P("row", "col"), P(), P(), P(), P(), P(), P())
    return jax.shard_map(
        local, mesh=mesh, in_specs=placed, out_specs=P("row", "col"), check_vma=False
    )
```

profile of v0, /device:TPU:1, one launch (start us, length us, event | category | flops | bytes accessed | tf_op | source)
XLA Modules:
  0.0 253.9 jit_solution(11986677601947028953)
XLA Ops:
  6.5 0.7 all-gather.7.cloned.1.call-update
  7.3 0.7 all-gather.5.cloned.1.call-update
  8.0 1.3 slice.33
  9.4 0.1 compare_reduce_fusion.9
  9.5 0.1 compare_reduce_fusion.11
  9.5 0.1 compare_reduce_fusion.13
  9.6 0.1 compare_reduce_fusion.15
  9.6 2.1 fusion.16
  11.7 4.4 %fusion.11 = (s32[750]{0:T(1024)S(1)}, s32[750]{0:T(1024)S(1)}) fusion(s32[]{:T(128)} %bitcast.28, s32[]{:T(128)} %bitcast.29, s32[]{:T(128)} %bitcast.30, s32[]{:T(128)} %bitcast.31, s32[]{:T(128)} %bitcast.32, s32[]{:T(128)} %bitcast.34, s32[]{:T(128)} %bitcast.33, s32[]{:T(128)S(6)} %mul.7), kind=kLoop, calls=%fused_computation.89 | loop fusion | flops 23250 | bytes 6032 | tf_op jit(solution)/shard_map/jit(_take)/gather | solution.py:27
  16.2 8.2 %select_select_fusion = s32[750]{0:T(1024)S(1)} fusion(pred[750]{0:T(1024)(128)(4,1)S(1)} %get-tuple-element.36, pred[750]{0:T(1024)(128)(4,1)S(1)} %get-tuple-element.37, pred[750]{0:T(1024)(128)(4,1)S(1)} %get-tuple-element.38, pred[750]{0:T(1024)(128)(4,1)S(1)} %get-tuple-element.39, pred[750]{0:T(1024)(128)(4,1)S(1)} %get-tuple-element.40, ...), kind=kLoop, calls=%fused_computation.65 | loop fusion | flops 9750 | bytes 15802 | tf_op jit(solution)/shard_map/jit(_take)/gather | solution.py:27
  24.4 4.8 %gather_fusion.4 = f32[750]{0:T(1024)S(1)} fusion(f32[200]{0:T(256)} %param.10, s32[1024]{0:T(1024)S(1)} %pad_clamp_fusion.2), kind=kCustom, calls=%fused_computation.4 | custom fusion | bytes 9000 | tf_op jit(solution)/shard_map/jit(_take)/gather | solution.py:30
  29.2 0.1 compare_reduce_fusion
  29.3 0.1 compare_reduce_fusion.1
  29.3 0.1 compare_reduce_fusion.2
  29.4 0.1 compare_reduce_fusion.3
  29.4 0.1 compare_reduce_fusion.4
  29.5 1.8 fusion.15
  31.3 4.5 %compare_select_fusion.6 = s32[900,1]{0,1:T(1,128)S(1)} fusion(s32[]{:T(128)} %bitcast.5, s32[]{:T(128)} %bitcast.6, s32[]{:T(128)} %bitcast.7, s32[]{:T(128)} %bitcast.8, s32[]{:T(128)} %bitcast.9, s32[]{:T(128)} %bitcast.11, s32[]{:T(128)} %bitcast.10, s32[]{:T(128)S(6)} %mul.6), kind=kLoop, calls=%fused_computation.20 | loop fusion | flops 21600 | bytes 3632 | tf_op jit(solution)/shard_map/jit(_take)/gather | solution.py:25
  35.7 3.1 %select_select_fusion.1 = s32[900]{0:T(1024)S(1)} fusion(pred[900]{0:T(1024)(128)(4,1)S(1)} %compare_reduce_fusion, pred[900]{0:T(1024)(128)(4,1)S(1)} %compare_reduce_fusion.1, pred[900]{0:T(1024)(128)(4,1)S(1)} %compare_reduce_fusion.2, pred[900]{0:T(1024)(128)(4,1)S(1)} %compare_reduce_fusion.3, pred[900]{0:T(1024)(128)(4,1)S(1)} %compare_reduce_fusion.4, ...), kind=kLoop, calls=%fused_computation.66 | loop fusion | flops 4500 | bytes 11720 | tf_op jit(solution)/shard_map/jit(_take)/gather | solution.py:25
  38.8 0.1 compare_select_fusion
  38.9 6.5 %gather_fusion.2 = f32[900]{0:T(1024)S(1)} fusion(f32[200]{0:T(256)S(1)} %copy-done.1, s32[1024]{0:T(1024)S(1)} %pad_clamp_fusion.3), kind=kCustom, calls=%fused_computation.2 | custom fusion | bytes 10800 | tf_op jit(solution)/shard_map/jit(_take)/gather | solution.py:29
  45.4 5.0 %gather_fusion.1 = s32[750]{0:T(1024)S(1)} fusion(s32[200]{0:T(256)S(1)} %copy-done.2, s32[1024]{0:T(1024)S(1)} %pad_clamp_fusion.2), kind=kCustom, calls=%fused_computation.1 | custom fusion | bytes 9000 | tf_op jit(solution)/shard_map/jit(_take)/gather | solution.py:32
  50.4 6.5 %gather_fusion = s32[900]{0:T(1024)S(1)} fusion(s32[200]{0:T(256)S(1)} %copy-done.2, s32[1024]{0:T(1024)S(1)} %pad_clamp_fusion.3), kind=kCustom, calls=%fused_computation | custom fusion | bytes 10800 | tf_op jit(solution)/shard_map/jit(_take)/gather | solution.py:31
  56.9 4.5 %gather_fusion.5 = f32[750]{0:T(1024)S(1)} fusion(f32[1200]{0:T(1024)S(1)} %copy-done, s32[1024]{0:T(1024)S(1)} %pad_clamp_fusion), kind=kCustom, calls=%fused_computation.5 | custom fusion | bytes 9000 | tf_op jit(solution)/shard_map/jit(_take)/gather | solution.py:30
  61.4 5.9 %gather_fusion.3 = f32[900]{0:T(1024)S(1)} fusion(f32[1200]{0:T(1024)S(1)} %copy-done, s32[1024]{0:T(1024)S(1)} %pad_clamp_fusion.1), kind=kCustom, calls=%fused_computation.3 | custom fusion | bytes 10800 | tf_op jit(solution)/shard_map/jit(_take)/gather | solution.py:29
  67.3 0.1 convert_reduce_fusion.1
  67.4 0.1 convert_reduce_fusion
  67.6 1.7 all-gather.7.cloned.1.call-done
  69.3 6.8 %reshape.467 = f32[2400,750]{1,0:T(8,128)} reshape(f32[16,150,750]{2,1,0:T(8,128)} %all-gather.7.cloned.1.call-done) | data formatting | bytes 14400000
  76.1 109.9 %all-gather.5.cloned.1.call-done = f32[32,75,900]{2,1,0:T(8,128)} async-done(((f32[1,75,900]{2,1,0:T(8,128)}), f32[32,75,900]{2,1,0:T(8,128)}) %all-gather.5.cloned.1.call-update) | async-done | bytes 8640016 | tf_op jit(solution)/shard_map/all_gather | solution.py:18
  186.0 8.2 %reshape.465 = f32[2400,900]{1,0:T(8,128)} reshape(f32[32,75,900]{2,1,0:T(8,128)} %all-gather.5.cloned.1.call-done) | data formatting | bytes 17280000
  194.3 52.8 %divide_select_fusion = f32[900,750]{1,0:T(8,128)} fusion(f32[2400,900]{1,0:T(8,128)} %reshape.465, f32[2400,750]{1,0:T(8,128)} %reshape.467, f32[750]{0:T(1024)S(1)} %select_subtract_fusion, f32[900]{0:T(1024)S(1)} %select_subtract_fusion.1, s32[750]{0:T(1024)S(1)} %add_xor_fusion, s32[900]{0:T(1024)S(1)} %add_xor_fusion.1), kind=kOutput, calls=%fused_computation.6 | convolution fusion | flops 19442702336 | bytes 18553200 | tf_op jit(solution)/shard_map/dot_general | solution.py:17
  (24 shorter events, 0.4 us)
Async XLA Ops:
  6.5 50.4 %copy-start = (f32[1200]{0:T(1024)S(1)}, f32[1200]{0:T(1024)}, u32[]{:S(2)}) copy-start(f32[1200]{0:T(1024)} %param.11) | copy-start | bytes 14404
  6.5 32.3 %copy-start.1 = (f32[200]{0:T(256)S(1)}, f32[200]{0:T(256)}, u32[]{:S(2)}) copy-start(f32[200]{0:T(256)} %param.10) | copy-start | bytes 2404
  6.5 38.9 %copy-start.2 = (s32[200]{0:T(256)S(1)}, s32[200]{0:T(256)}, u32[]{:S(2)}) copy-start(s32[200]{0:T(256)} %param.12) | copy-start | bytes 2404
  6.5 62.8 %all-gather.7.cloned.1.call-start = ((), (), s32[]{:S(2)}) async-start(), calls=%async_computation.1 | async-start | bytes 7938048 | tf_op jit(solution)/shard_map/all_gather | solution.py:16
  7.3 178.8 %all-gather.5.cloned.1.call-start = ((), (), s32[]{:S(2)}) async-start(), calls=%async_computation | async-start | bytes 10813440 | tf_op jit(solution)/shard_map/all_gather | solution.py:18
  45.4 21.9 %copy-start.3 = (s32[8]{0:T(128)S(1)}, s32[8]{0:T(128)}, u32[]{:S(2)}) copy-start(s32[8]{0:T(128)} %param.15) | copy-start | bytes 100
Sparse Core Ops, SparseCore 0:
  9.5 59.7 all-gather.6
  72.5 113.4 all-gather.4
where the time goes:
time: 254 us
  waiting for transfers between devices  113 us (44%)
  local copies, waits for them, and re-layouts  53.2 us (21%)
  matrix products  52.8 us (21%)
  other arithmetic  21.1 us (8%)
  between operations  13.6 us (5%)
    all_gather x1, waiting for transfers between devices, local(): lax.all_gather(lam, 'col', axis=1, tiled=True)  110 us
    dot_general x1, matrix products, local(): jnp.dot(lax.all_gather(lam, 'col', axis=1, tiled=True), cycle_full, preci...  52.8 us
    unnamed x10, local copies, waits for them, and re-layouts  15 us
    gather x9, other arithmetic, local(): occ_col = jnp.take(pair_occ, cols // V)  12.9 us
    gather x2, local copies, waits for them, and re-layouts, local(): row_energy = jnp.take(eps_occ, occ_row) - jnp.take(eps_vir, vir_row)  12.3 us
    gather x2, local copies, waits for them, and re-layouts, local(): col_energy = jnp.take(eps_occ, occ_col) - jnp.take(eps_vir, vir_col)  9.27 us
    gather x7, other arithmetic, local(): occ_row = jnp.take(slab, rows // V)  7.81 us
    gather x1, local copies, waits for them, and re-layouts, local(): jnp.take(occ_irrep, occ_row)  6.49 us
  transfers between devices with their start and end apart: 2, of which 2 were waited for; matrix products, arithmetic and copies ran while one was open for 26% of the time, Pallas kernels for 0%

commit v1 on v0

--- a/solution.py
+++ b/solution.py
@@ -15,7 +15,9 @@
     col_count = cycle.shape[1]
     cycle_full = lax.all_gather(cycle, "row", axis=0, tiled=True)
     prod = jnp.dot(
-        lax.all_gather(lam, "col", axis=1, tiled=True),
+        jnp.concatenate(
+            lax.all_to_all(jnp.stack([lam] * lax.axis_size("col")), "col", 0, 0), axis=1
+        ),
         cycle_full,
         precision=lax.Precision.HIGHEST,
         preferred_element_type=jnp.float32,

time: 254 us -> 337 us (1.33); the launches traced: 254 us -> 333 us
  waiting for transfers between devices: 113 us -> 174 us
  starting transfers between devices: 0.04 us -> 14 us
    all_to_all x0 -> x1, waiting for transfers between devices: none -> 173 us  [local(): lax.all_to_all(jnp.stack([lam] * lax.axis_size('col')), 'col', 0, 0)]
    all_gather x1 -> x0, waiting for transfers between devices: 110 us -> none  [local(): lax.all_gather(lam, 'col', axis=1, tiled=True)]
    all_to_all x0 -> x1, starting transfers between devices: none -> 14 us  [local(): lax.all_to_all(jnp.stack([lam] * lax.axis_size('col')), 'col', 0, 0)]
    unnamed x10 -> x13, local copies, waits for them, and re-layouts: 15 us -> 6.71 us
    reshape x0 -> x1, local copies, waits for them, and re-layouts: none -> 8.22 us  [local(): jnp.concatenate(lax.all_to_all(jnp.stack([lam] * lax.axis_size('col')), '...]
    another operation x0 -> x1, local copies, waits for them, and re-layouts: none -> 6.15 us  [local(): jnp.stack([lam] * lax.axis_size('col'))]
  transfers between devices with their start and end apart: 2 -> 2, of which waited for: 2 -> 2; matrix products, arithmetic and copies ran while one was open for 26% -> 19% of each run, Pallas kernels for 0% -> 0%
where the time goes in v1:
time: 337 us; the launch traced here: 333 us
  waiting for transfers between devices  174 us (52%)
  local copies, waits for them, and re-layouts  56.4 us (17%)
  matrix products  52.8 us (16%)
  other arithmetic  21.3 us (6%)
  starting transfers between devices  14 us (4%)
  between operations  13.6 us (4%)
    all_to_all x1, waiting for transfers between devices, local(): lax.all_to_all(jnp.stack([lam] * lax.axis_size('col')), 'col', 0, 0)  173 us
    dot_general x1, matrix products, local(): jnp.dot(jnp.concatenate(lax.all_to_all(jnp.stack([lam] * lax.axis_size('c...  52.8 us
    all_to_all x1, starting transfers between devices, local(): lax.all_to_all(jnp.stack([lam] * lax.axis_size('col')), 'col', 0, 0)  14 us
    gather x9, other arithmetic, local(): occ_col = jnp.take(pair_occ, cols // V)  13 us
    gather x2, local copies, waits for them, and re-layouts, local(): row_energy = jnp.take(eps_occ, occ_row) - jnp.take(eps_vir, vir_row)  12.3 us
    gather x2, local copies, waits for them, and re-layouts, local(): col_energy = jnp.take(eps_occ, occ_col) - jnp.take(eps_vir, vir_col)  9.45 us
    reshape x1, local copies, waits for them, and re-layouts, local(): jnp.concatenate(lax.all_to_all(jnp.stack([lam] * lax.axis_size('col')), '...  8.22 us
    gather x7, other arithmetic, local(): occ_row = jnp.take(slab, rows // V)  7.91 us
  transfers between devices with their start and end apart: 2, of which 2 were waited for; matrix products, arithmetic and copies ran while one was open for 19% of the time, Pallas kernels for 0%

profile of v1, /device:TPU:1, one launch (start us, length us, event | category | flops | bytes accessed | tf_op | source)
XLA Modules:
  0.0 332.6 jit_solution(18395835799524052855)
XLA Ops:
  6.5 6.2 %stack.2 = f32[32,900,75]{1,2,0:T(8,128)} broadcast(f32[900,75]{0,1:T(8,128)} %param.8), dimensions={1,2} | broadcast | bytes 8910000 | tf_op jit(solution)/shard_map/stack | solution.py:19
  12.7 14.0 %all-to-all-start = ((f32[32,900,75]{1,2,0:T(8,128)}), f32[32,900,75]{1,2,0:T(8,128)}, u32[]{:S(2)}, u32[]{:S(2)}) async-start(f32[32,900,75]{1,2,0:T(8,128)} %stack.2), calls=%async_computation | async-start | bytes 20971520 | tf_op jit(solution)/shard_map/all_to_all | solution.py:19
  26.7 0.7 all-gather.3.cloned.1.call-update
  27.4 0.7 slice.33
  28.2 0.1 compare_reduce_fusion.9
  28.3 0.1 compare_reduce_fusion.11
  28.3 0.1 compare_reduce_fusion.13
  28.5 0.7 fusion.16
  29.2 4.4 %fusion.11 = (s32[750]{0:T(1024)S(1)}, s32[750]{0:T(1024)S(1)}) fusion(s32[]{:T(128)} %bitcast.28, s32[]{:T(128)} %bitcast.29, s32[]{:T(128)} %bitcast.30, s32[]{:T(128)} %bitcast.31, s32[]{:T(128)} %bitcast.32, s32[]{:T(128)} %bitcast.34, s32[]{:T(128)} %bitcast.33, s32[]{:T(128)S(6)} %mul.7), kind=kLoop, calls=%fused_computation.89 | loop fusion | flops 23250 | bytes 6032 | tf_op jit(solution)/shard_map/jit(_take)/gather | solution.py:29
  33.6 8.2 %select_select_fusion = s32[750]{0:T(1024)S(1)} fusion(pred[750]{0:T(1024)(128)(4,1)S(1)} %get-tuple-element.36, pred[750]{0:T(1024)(128)(4,1)S(1)} %get-tuple-element.37, pred[750]{0:T(1024)(128)(4,1)S(1)} %get-tuple-element.38, pred[750]{0:T(1024)(128)(4,1)S(1)} %get-tuple-element.39, pred[750]{0:T(1024)(128)(4,1)S(1)} %get-tuple-element.40, ...), kind=kLoop, calls=%fused_computation.65 | loop fusion | flops 9750 | bytes 15802 | tf_op jit(solution)/shard_map/jit(_take)/gather | solution.py:29
  41.9 5.0 %gather_fusion.4 = f32[750]{0:T(1024)S(1)} fusion(f32[200]{0:T(256)S(1)} %copy-done.1, s32[1024]{0:T(1024)S(1)} %pad_clamp_fusion.2), kind=kCustom, calls=%fused_computation.4 | custom fusion | bytes 9000 | tf_op jit(solution)/shard_map/jit(_take)/gather | solution.py:32
  46.9 0.1 compare_reduce_fusion
  46.9 0.1 compare_reduce_fusion.1
  47.0 0.1 compare_reduce_fusion.2
  47.0 0.1 compare_reduce_fusion.3
  47.1 0.1 compare_reduce_fusion.4
  47.1 0.7 fusion.15
  47.8 4.5 %compare_select_fusion.6 = s32[900,1]{0,1:T(1,128)S(1)} fusion(s32[]{:T(128)} %bitcast.5, s32[]{:T(128)} %bitcast.6, s32[]{:T(128)} %bitcast.7, s32[]{:T(128)} %bitcast.8, s32[]{:T(128)} %bitcast.9, s32[]{:T(128)} %bitcast.11, s32[]{:T(128)} %bitcast.10, s32[]{:T(128)S(6)} %mul.6), kind=kLoop, calls=%fused_computation.20 | loop fusion | flops 21600 | bytes 3632 | tf_op jit(solution)/shard_map/jit(_take)/gather | solution.py:27
  52.3 3.2 select_select_fusion.1
  55.5 0.1 compare_select_fusion
  55.6 6.5 %gather_fusion.2 = f32[900]{0:T(1024)S(1)} fusion(f32[200]{0:T(256)S(1)} %copy-done.1, s32[1024]{0:T(1024)S(1)} %pad_clamp_fusion.3), kind=kCustom, calls=%fused_computation.2 | custom fusion | bytes 10800 | tf_op jit(solution)/shard_map/jit(_take)/gather | solution.py:31
  62.1 5.0 %gather_fusion.1 = s32[750]{0:T(1024)S(1)} fusion(s32[200]{0:T(256)S(1)} %copy-done.2, s32[1024]{0:T(1024)S(1)} %pad_clamp_fusion.2), kind=kCustom, calls=%fused_computation.1 | custom fusion | bytes 9000 | tf_op jit(solution)/shard_map/jit(_take)/gather | solution.py:34
  67.1 6.5 %gather_fusion = s32[900]{0:T(1024)S(1)} fusion(s32[200]{0:T(256)S(1)} %copy-done.2, s32[1024]{0:T(1024)S(1)} %pad_clamp_fusion.3), kind=kCustom, calls=%fused_computation | custom fusion | bytes 10800 | tf_op jit(solution)/shard_map/jit(_take)/gather | solution.py:33
  73.6 4.5 %gather_fusion.5 = f32[750]{0:T(1024)S(1)} fusion(f32[1200]{0:T(1024)S(1)} %copy-done, s32[1024]{0:T(1024)S(1)} %pad_clamp_fusion), kind=kCustom, calls=%fused_computation.5 | custom fusion | bytes 9000 | tf_op jit(solution)/shard_map/jit(_take)/gather | solution.py:32
  78.1 5.9 %gather_fusion.3 = f32[900]{0:T(1024)S(1)} fusion(f32[1200]{0:T(1024)S(1)} %copy-done, s32[1024]{0:T(1024)S(1)} %pad_clamp_fusion.1), kind=kCustom, calls=%fused_computation.3 | custom fusion | bytes 10800 | tf_op jit(solution)/shard_map/jit(_take)/gather | solution.py:31
  84.0 0.1 convert_reduce_fusion.1
  84.1 0.1 convert_reduce_fusion
  84.3 1.2 all-gather.3.cloned.1.call-done
  85.5 6.7 %reshape.475 = f32[2400,750]{1,0:T(8,128)} reshape(f32[16,150,750]{2,1,0:T(8,128)} %all-gather.3.cloned.1.call-done) | data formatting | bytes 14400000
  92.2 172.5 %all-to-all-done = f32[32,900,75]{1,2,0:T(8,128)} async-done(((f32[32,900,75]{1,2,0:T(8,128)}), f32[32,900,75]{1,2,0:T(8,128)}, u32[]{:S(2)}, u32[]{:S(2)}) %all-to-all-start) | async-done | bytes 8640032 | tf_op jit(solution)/shard_map/all_to_all | solution.py:19
  264.7 8.2 %reshape.305 = f32[900,2400]{0,1:T(8,128)} reshape(f32[900,32,75]{0,2,1:T(8,128)} %bitcast.35) | data formatting | bytes 17280000 | tf_op jit(solution)/shard_map/reshape | solution.py:18
  272.9 52.8 %divide_select_fusion = f32[900,750]{1,0:T(8,128)} fusion(f32[900,2400]{0,1:T(8,128)} %reshape.305, f32[2400,750]{1,0:T(8,128)} %reshape.475, f32[750]{0:T(1024)S(1)} %select_subtract_fusion, f32[900]{0:T(1024)S(1)} %select_subtract_fusion.1, s32[750]{0:T(1024)S(1)} %add_xor_fusion, s32[900]{0:T(1024)S(1)} %add_xor_fusion.1), kind=kOutput, calls=%fused_computation.6 | convolution fusion | flops 19442702336 | bytes 18553200 | tf_op jit(solution)/shard_map/dot_general | solution.py:17
  (28 shorter events, 0.5 us)
Async XLA Ops:
  6.5 67.1 %copy-start = (f32[1200]{0:T(1024)S(1)}, f32[1200]{0:T(1024)}, u32[]{:S(2)}) copy-start(f32[1200]{0:T(1024)} %param.11) | copy-start | bytes 14404
  12.7 14.7 %copy-start.3 = (s32[20]{0:T(128)S(1)}, s32[20]{0:T(128)}, u32[]{:S(2)}) copy-start(s32[20]{0:T(128)} %param.14) | copy-start | bytes 244
  12.7 29.2 %copy-start.1 = (f32[200]{0:T(256)S(1)}, f32[200]{0:T(256)}, u32[]{:S(2)}) copy-start(f32[200]{0:T(256)} %param.10) | copy-start | bytes 2404
  12.7 34.5 %copy-start.4 = (s32[12]{0:T(128)S(1)}, s32[12]{0:T(128)}, u32[]{:S(2)}) copy-start(s32[12]{0:T(128)} %param.13) | copy-start | bytes 148
  12.7 252.0 %all-to-all-start = ((f32[32,900,75]{1,2,0:T(8,128)}), f32[32,900,75]{1,2,0:T(8,128)}, u32[]{:S(2)}, u32[]{:S(2)}) async-start(f32[32,900,75]{1,2,0:T(8,128)} %stack.2), calls=%async_computation | async-start | bytes 20971520 | tf_op jit(solution)/shard_map/all_to_all | solution.py:19
  26.7 35.4 %copy-start.2 = (s32[200]{0:T(256)S(1)}, s32[200]{0:T(256)}, u32[]{:S(2)}) copy-start(s32[200]{0:T(256)} %param.12) | copy-start | bytes 2404
  26.7 58.8 %all-gather.3.cloned.1.call-start = ((), (), s32[]{:S(2)}) async-start(), calls=%async_computation.1 | async-start | bytes 7938048 | tf_op jit(solution)/shard_map/all_gather | solution.py:16
  62.1 21.9 %copy-start.5 = (s32[8]{0:T(128)S(1)}, s32[8]{0:T(128)}, u32[]{:S(2)}) copy-start(s32[8]{0:T(128)} %param.15) | copy-start | bytes 100
Sparse Core Ops, SparseCore 0:
  29.6 55.8 all-gather.2
